TPU v7x, 32 devices: a whole 2x2x4 slice. The times are simulated.
32 devices in a mesh: orb: 32 (over z, y, x, core).
Axes of the slice: x: 2, y: 2, z: 4, core: 2. Of those that a mesh axis runs over, the one named last changes fastest.
Arguments:
- orbitals: bfloat16 [128, 64, 4096], P('orb'), may hold values from -6 to 6
- pair_list: int32 [512, 2], P('orb'), may hold values from 0 to 15, as said below
- pair_counts: int32 [32], P('orb'), may hold values from 1 to 16, as said below
Outputs:
- exchange_field: float32 [128, 64, 4096], P('orb')
Inputs may be any that keep to these rules, and one draw needn't show every extreme that they name: `pair_list`: in each row (a, w) of a device's block, a is one of its own 4 orbitals and w is below (4) * 4; where w < 4 both orbitals are the device's own and w >= a. The rows of one device's block are distinct. `pair_counts`: some device's count is 16; rows past a device's count are not used.
All inputs are finite; a program needn't handle non-finite values.
Results may differ from a plain program's by a relative error of at most 0.0003.
Values may be sent and summed in bfloat16 or wider, within the bound.
No kernel may reach another device: no remote copies, remote signals or barrier semaphores. Data moves between devices by JAX's collectives and lax.ppermute only.
A program may use at most 128 MiB of HBM per device.

v0:
```python
import functools
import math

import jax
import jax.numpy as jnp
from jax import lax
from jax.sharding import PartitionSpec as P

REACH = 3


screening = 0.5


def passed_along(value, axis, steps):
    count = lax.axis_size(axis)
    pairs = [(source, (source + steps) % count) for source in range(count)]
    return lax.ppermute(value, axis, pairs)


def sine_table(points):
    modes = jnp.arange(points, dtype=jnp.float32) + 1.0
    return jnp.sin(math.pi * modes[:, None] * modes[None, :] / (points + 1))


def inverse_denominators(points):
    modes = jnp.arange(points, dtype=jnp.float32) + 1.0
    eigen = 4.0 * jnp.sin(math.pi * modes / (2.0 * (points + 1))) ** 2
    total = eigen[:, None, None] + eigen[None, :, None] + eigen[None, None, :] + screening
    return ((2.0 / (points + 1)) ** 3 / total).reshape(points, points * points)


def sine_cube(fields, sines):
    points = sines.shape[0]
    cube = fields.reshape(points, points, points)
    highest = lax.Precision.HIGHEST
    cube = jnp.einsum("kx,xyz->kyz", sines, cube, precision=highest)
    cube = jnp.einsum("ky,xyz->xkz", sines, cube, precision=highest)
    cube = jnp.einsum("kz,xyz->xyk", sines, cube, precision=highest)
    return cube.reshape(points, points * points)


def screened_potential(density, sines, inverse):
    return sine_cube(sine_cube(density, sines) * inverse, sines)


def pick_orbital(blocks, position):
    return lax.dynamic_index_in_dim(blocks, position, 0, keepdims=False).astype(jnp.float32)


def near_blocks(orbitals, direction):
    return [passed_along(orbitals, "orb", direction * distance) for distance in range(1, REACH + 1)]


def visit_pair(window, pair_list, own_count, only_own, sines, inverse, slot, totals):
    own_index = pair_list[slot, 0]
    other_index = pair_list[slot, 1]
    one_side = pick_orbital(window, own_index)
    other_side = pick_orbital(window, other_index)
    potential = screened_potential(one_side * other_side, sines, inverse)
    totals = totals.at[own_index].add(potential * other_side)
    weight = (other_index != own_index).astype(jnp.float32)
    return totals.at[other_index].add(potential * one_side * weight)


def shards(orbitals, pair_list, pair_counts):
    own_count = orbitals.shape[0]
    box_side = orbitals.shape[1]
    sines = sine_table(box_side)
    inverse = inverse_denominators(box_side)
    live_count = pair_counts[0]
    ahead_blocks = near_blocks(orbitals, -1)
    window = jnp.concatenate([orbitals] + ahead_blocks, 0)
    totals = jnp.zeros((window.shape[0],) + orbitals.shape[1:], jnp.float32)
    stepper = functools.partial(visit_pair, window, pair_list, own_count, False, sines, inverse)
    totals = lax.fori_loop(0, live_count, stepper, totals)
    fields = totals[:own_count]
    for distance in range(1, REACH + 1):
        returned = passed_along(
            totals[distance * own_count : (distance + 1) * own_count], "orb", distance
        )
        fields = fields + returned
    return -fields


def solution(mesh):
    return jax.shard_map(
        shards,
        mesh=mesh,
        in_specs=(P("orb", None, None), P("orb", None), P("orb")),
        out_specs=P("orb", None, None),
        check_vma=False,
    )
```

profile of v0, /device:TPU:17, one launch (start us, length us, event | category | flops | bytes accessed | tf_op | source)
XLA Modules:
  0.0 1340.8 jit_solution(13960997471071826803)
XLA Ops:
  4.0 65.1 %collective-permute-done.1 = bf16[4,64,4096]{2,1,0:T(8,128)(2,1)S(1)} collective-permute-done((bf16[4,64,4096]{2,1,0:T(8,128)(2,1)}, bf16[4,64,4096]{2,1,0:T(8,128)(2,1)S(1)}, u32[]{:S(2)}, u32[]{:S(2)}) %collective-permute-start.1) | collective-permute-done | bytes 2097184 | tf_op jit(solution)/shard_map/ppermute | solution.py:18
  69.0 23.6 %collective-permute-done = bf16[4,64,4096]{2,1,0:T(8,128)(2,1)} collective-permute-done((bf16[4,64,4096]{2,1,0:T(8,128)(2,1)}, bf16[4,64,4096]{2,1,0:T(8,128)(2,1)}, u32[]{:S(2)}, u32[]{:S(2)}) %collective-permute-start) | collective-permute-done | bytes 2097184 | tf_op jit(solution)/shard_map/ppermute | solution.py:18
  92.6 21.4 %collective-permute-done.2 = bf16[4,64,4096]{2,1,0:T(8,128)(2,1)} collective-permute-done((bf16[4,64,4096]{2,1,0:T(8,128)(2,1)}, bf16[4,64,4096]{2,1,0:T(8,128)(2,1)}, u32[]{:S(2)}, u32[]{:S(2)}) %collective-permute-start.2) | collective-permute-done | bytes 2097184 | tf_op jit(solution)/shard_map/ppermute | solution.py:18
  114.0 6.6 pad_maximum_fusion
  120.6 7.8 broadcast_in_dim.2
  128.4 288.6 %while.14 = (s32[]{:T(128)}, f32[16,64,4096]{2,1,0:T(8,128)}, s32[]{:T(128)}, s32[16,2]{0,1:T(2,128)S(1)}, bf16[16,64,4096]{2,1,0:T(8,128)(2,1)}, /*index=5*/f32...) while((s32[]{:T(128)}, f32[16,64,4096]{2,1,0:T(8,128)}, ...), condition=%wide.region_3.4_spmd.clone.clone, body=%wide.region_0.3_spmd.clone.clone.sunk | while | flops 1212203008 | bytes 38836536 | solution.py:76
  140.7 4.2 copy.19
  156.8 5.2 fusion.87
  161.9 4.3 fusion.88
  169.3 7.8 fusion.89
  198.2 4.2 copy.19
  214.3 5.2 fusion.87
  219.5 4.3 fusion.88
  226.9 7.8 fusion.89
  255.8 4.2 copy.19
  271.9 5.2 fusion.87
  277.0 4.3 fusion.88
  284.4 7.8 fusion.89
  313.4 4.2 copy.19
  329.5 5.2 fusion.87
  334.6 4.3 fusion.88
  342.0 7.8 fusion.89
  371.0 4.2 copy.19
  387.0 5.2 fusion.87
  392.2 4.3 fusion.88
  399.6 7.8 fusion.89
  417.1 9.7 fusion.51
  426.8 36.9 %collective-permute-start.5 = (f32[4,64,4096]{2,1,0:T(8,128)}, f32[4,64,4096]{2,1,0:T(8,128)S(1)}, u32[]{:S(2)}, u32[]{:S(2)}) collective-permute-start(f32[4,64,4096]{2,1,0:T(8,128)} %get-tuple-element.155), channel_id=1, source_target_pairs={{0,3},{1,4},{2,5},{3,6},{4,7},{5,8},{6,9},{7,10},{8,11},{9,12},{10... | collective-permute-start | bytes 12582920 | tf_op jit(solution)/shard_map/ppermute | solution.py:18
  463.7 602.0 %collective-permute-start.4 = (f32[4,64,4096]{2,1,0:T(8,128)}, f32[4,64,4096]{2,1,0:T(8,128)S(1)}, u32[]{:S(2)}, u32[]{:S(2)}) collective-permute-start(f32[4,64,4096]{2,1,0:T(8,128)} %get-tuple-element.156), channel_id=1, source_target_pairs={{0,2},{1,3},{2,4},{3,5},{4,6},{5,7},{6,8},{7,9},{8,10},{9,11},{10,... | collective-permute-start | bytes 12582920 | tf_op jit(solution)/shard_map/ppermute | solution.py:18
  1065.7 135.2 %collective-permute-done.5 = f32[4,64,4096]{2,1,0:T(8,128)S(1)} collective-permute-done((f32[4,64,4096]{2,1,0:T(8,128)}, f32[4,64,4096]{2,1,0:T(8,128)S(1)}, u32[]{:S(2)}, u32[]{:S(2)}) %collective-permute-start.5) | collective-permute-done | bytes 4194336 | tf_op jit(solution)/shard_map/ppermute | solution.py:18
  1200.9 134.2 %collective-permute-done.4 = f32[4,64,4096]{2,1,0:T(8,128)S(1)} collective-permute-done((f32[4,64,4096]{2,1,0:T(8,128)}, f32[4,64,4096]{2,1,0:T(8,128)S(1)}, u32[]{:S(2)}, u32[]{:S(2)}) %collective-permute-start.4) | collective-permute-done | bytes 4194336 | tf_op jit(solution)/shard_map/ppermute | solution.py:18
  1335.0 5.8 add_negate_fusion
  (89 shorter events, 155.2 us)
Async XLA Ops:
  0.0 69.0 %collective-permute-start.1 = (bf16[4,64,4096]{2,1,0:T(8,128)(2,1)}, bf16[4,64,4096]{2,1,0:T(8,128)(2,1)S(1)}, u32[]{:S(2)}, u32[]{:S(2)}) collective-permute-start(bf16[4,64,4096]{2,1,0:T(8,128)(2,1)} %param.9), channel_id=1, source_target_pairs={{0,30},{1,31},{2,0},{3,1},{4,2},{5,3},{6,4},{7,5},{8,6},{9,7},{10,... | collective-permute-start | bytes 6291464 | tf_op jit(solution)/shard_map/ppermute | solution.py:18
  2.1 90.6 %collective-permute-start = (bf16[4,64,4096]{2,1,0:T(8,128)(2,1)}, bf16[4,64,4096]{2,1,0:T(8,128)(2,1)}, u32[]{:S(2)}, u32[]{:S(2)}) collective-permute-start(bf16[4,64,4096]{2,1,0:T(8,128)(2,1)} %param.9), channel_id=1, source_target_pairs={{0,31},{1,0},{2,1},{3,2},{4,3},{5,4},{6,5},{7,6},{8,7},{9,8},{10,9... | collective-permute-start | bytes 6291464 | tf_op jit(solution)/shard_map/ppermute | solution.py:18
  3.0 111.0 %collective-permute-start.2 = (bf16[4,64,4096]{2,1,0:T(8,128)(2,1)}, bf16[4,64,4096]{2,1,0:T(8,128)(2,1)}, u32[]{:S(2)}, u32[]{:S(2)}) collective-permute-start(bf16[4,64,4096]{2,1,0:T(8,128)(2,1)} %param.9), channel_id=1, source_target_pairs={{0,29},{1,30},{2,31},{3,0},{4,1},{5,2},{6,3},{7,4},{8,5},{9,6},{10... | collective-permute-start | bytes 6291464 | tf_op jit(solution)/shard_map/ppermute | solution.py:18
  120.6 7.8 copy-start
  120.6 7.8 copy-start.1
  426.8 638.9 %collective-permute-start.3 = (f32[4,64,4096]{2,1,0:T(8,128)}, f32[4,64,4096]{2,1,0:T(8,128)S(1)}, u32[]{:S(2)}, u32[]{:S(2)}) collective-permute-start(f32[4,64,4096]{2,1,0:T(8,128)} %get-tuple-element.154), channel_id=1, source_target_pairs={{0,1},{1,2},{2,3},{3,4},{4,5},{5,6},{6,7},{7,8},{8,9},{9,10},{10,1... | collective-permute-start | bytes 12582920 | tf_op jit(solution)/shard_map/ppermute | solution.py:18
  426.8 774.1 %collective-permute-start.5 = (f32[4,64,4096]{2,1,0:T(8,128)}, f32[4,64,4096]{2,1,0:T(8,128)S(1)}, u32[]{:S(2)}, u32[]{:S(2)}) collective-permute-start(f32[4,64,4096]{2,1,0:T(8,128)} %get-tuple-element.155), channel_id=1, source_target_pairs={{0,3},{1,4},{2,5},{3,6},{4,7},{5,8},{6,9},{7,10},{8,11},{9,12},{10... | collective-permute-start | bytes 12582920 | tf_op jit(solution)/shard_map/ppermute | solution.py:18
  463.7 871.3 %collective-permute-start.4 = (f32[4,64,4096]{2,1,0:T(8,128)}, f32[4,64,4096]{2,1,0:T(8,128)S(1)}, u32[]{:S(2)}, u32[]{:S(2)}) collective-permute-start(f32[4,64,4096]{2,1,0:T(8,128)} %get-tuple-element.156), channel_id=1, source_target_pairs={{0,2},{1,3},{2,4},{3,5},{4,6},{5,7},{6,8},{7,9},{8,10},{9,11},{10,... | collective-permute-start | bytes 12582920 | tf_op jit(solution)/shard_map/ppermute | solution.py:18
where the time goes:
time: 1330 us; the launch traced here: 1340 us
  starting transfers between devices  643 us (48%)
  waiting for transfers between devices  379 us (28%)
  matrix products  131 us (10%)
  local copies, waits for them, and re-layouts  98.7 us (7%)
  other arithmetic  59.6 us (4%)
  loops' own time  29.7 us (2%)
    ppermute x6, starting transfers between devices, passed_along(): return lax.ppermute(value, axis, pairs)  643 us
    ppermute x6, waiting for transfers between devices, passed_along(): return lax.ppermute(value, axis, pairs)  379 us
    dot_general x10, matrix products, sine_cube(): cube = jnp.einsum('ky,xyz->xkz', sines, cube, precision=highest)  56.9 us
    dot_general x10, matrix products, sine_cube(): cube = jnp.einsum('kx,xyz->kyz', sines, cube, precision=highest)  38.2 us
    dot_general x10, local copies, waits for them, and re-layouts, sine_cube(): cube = jnp.einsum('kx,xyz->kyz', sines, cube, precision=highest)  36.1 us
    dot_general x10, matrix products, sine_cube(): cube = jnp.einsum('kz,xyz->xyk', sines, cube, precision=highest)  35.7 us
    another operation x1, loops' own time, shards(): totals = lax.fori_loop(0, live_count, stepper, totals)  29.7 us
  transfers between devices with their start and end apart: 6, of which 5 were waited for; matrix products, arithmetic and copies ran while one was open for 0% of the time, Pallas kernels for 0%

commit v1 on v0

v1 whole, which is shorter than its diff:
```python
import functools
import math

import jax
import jax.numpy as jnp
import numpy as np
from jax import lax
from jax.experimental import pallas as pl
from jax.experimental.pallas import tpu as pltpu
from jax.sharding import PartitionSpec as P

REACH = 3
LANES = 128
GROUP = 8
NOWHERE = 99

screening = 0.5


def routes(count):
    groups = count // GROUP

    def device(group, chip, core):
        return (group % groups) * GROUP + 2 * chip + core

    names = ("x1", "x2", "x3a", "x3b", "y1", "y2", "y3a", "y3b", "z1", "z2")
    table = {name: [] for name in names}
    for g in range(groups):
        for c in range(4):
            first = 1 if c in (0, 2) else 0
            table["x1"].append((device(g, c, first), device(g, c ^ 1, first)))
            table["x2"].append((device(g, c, 1 - first), device(g, c ^ 1, 1 - first)))
            near = 1 if c in (0, 1) else 0
            table["y1"].append((device(g, c, near), device(g, c ^ 2, 1 - near)))
            edge = 1 if c in (2, 3) else 0
            step = 1 if c in (2, 3) else -1
            table["z1"].append((device(g, c, edge), device(g + step, c, edge)))
            table["y2"].append((device(g, c, edge), device(g, c ^ 2, 1 - edge)))
        table["z2"] += [(device(g, 2, 0), device(g + 1, 2, 0)), (device(g, 1, 1), device(g - 1, 1, 1))]
        table["x3a"] += [(device(g, 0, 1), device(g, 1, 1)), (device(g, 3, 0), device(g, 2, 0))]
        table["x3b"] += [(device(g, 1, 0), device(g, 0, 0)), (device(g, 2, 1), device(g, 3, 1))]
        table["y3a"] += [(device(g, 0, 0), device(g, 2, 0)), (device(g, 3, 1), device(g, 1, 1))]
        table["y3b"] += [(device(g, 2, 0), device(g, 0, 0)), (device(g, 1, 1), device(g, 3, 1))]
    table["core"] = [(d, d ^ 1) for d in range(count)]
    for name in ("x1", "x2", "x3a", "x3b", "y3a", "y3b"):
        table[name + "s"] = [(target, target ^ 1) for _, target in table[name]]
    return table


HELD = {
    "x1": (2, 1, 6, 5),
    "x2": (3, 0, 7, 4),
    "x3": (-1, 4, 3, 8),
    "y1": (4, 6, 1, 3),
    "y2": (-3, -1, 8, 10),
    "y3": (-2, 5, 2, 9),
}
TAKER = {
    "x1": (0, 1, 0, 1),
    "x2": (1, 0, 1, 0),
    "x3": (0, 1, 0, 1),
    "y1": (1, 1, 0, 0),
    "y2": (0, 0, 1, 1),
    "y3": (0, 1, 0, 1),
}


def tables(points):
    modes = np.arange(points) + 1.0
    sines = np.sin(math.pi * np.outer(modes, modes) / (points + 1)) * math.sqrt(2.0 / (points + 1))
    high = sines.astype(jnp.bfloat16)
    low = (sines - high.astype(np.float64)).astype(jnp.bfloat16)
    high, low = high.astype(np.float32), low.astype(np.float32)
    none = np.zeros_like(high)

    def straight(t):
        return np.block([[t, none], [none, t]])

    def crossed(t):
        return np.block([[none, t], [t, none]])

    def spread(form):
        return np.block([[form(high), form(low)], [form(high), form(low)]])

    along_lines = np.stack([spread(straight), spread(crossed)]).astype(jnp.bfloat16)
    along_planes = np.concatenate([high, high, low, low], 1).astype(jnp.bfloat16)
    eigen = 4.0 * np.sin(math.pi * modes / (2.0 * (points + 1))) ** 2
    diagonal = 2.0 + eigen[:, None] + eigen[None, :] + screening
    ratios = [1.0 / diagonal]
    for _ in range(points // 2 - 1):
        ratios.append(1.0 / (diagonal - ratios[-1]))
    middle = 1.0 / (1.0 - ratios[-1] ** 2)
    ratios = np.stack(ratios)
    ratios = np.concatenate([ratios, ratios], 2).astype(np.float32)
    middle = np.concatenate([middle, middle], 1).astype(np.float32)
    return along_lines, along_planes, ratios, middle


def split(value):
    high = value.astype(jnp.bfloat16)
    return high, (value - high.astype(jnp.float32)).astype(jnp.bfloat16)


def dot(left, right):
    return jnp.dot(left, right, preferred_element_type=jnp.float32)


def sine_lines(value, weights):
    product = dot(jnp.concatenate(split(value), 1), weights)
    return product[:, :LANES] + product[:, LANES:]


def sine_planes(value, weights):
    high, low = split(value)
    return dot(weights, jnp.concatenate([high, low, high, low], 0))


def tile(index):
    if isinstance(index, int):
        return pl.ds(index * LANES, LANES)
    return pl.ds(pl.multiple_of(index * LANES, LANES), LANES)


def potential_tiles(load_left, load_right, give, lines_ref, planes_ref, ratios_ref, middle_ref, kept, points):
    couples = points // 4
    last = 2 * couples - 1
    first_half = lax.broadcasted_iota(jnp.int32, (points, LANES), 1) < points
    even, odd = [], []
    for i in range(couples):
        near = load_left(i).astype(jnp.float32) * load_right(i).astype(jnp.float32)
        far = load_left(last - i).astype(jnp.float32) * load_right(last - i).astype(jnp.float32)
        even.append(jnp.where(first_half, near, far))
        odd.append(jnp.where(first_half, far, near))
    even = sine_lines(jnp.concatenate(even, 0), lines_ref[0])
    odd = sine_lines(jnp.concatenate(odd, 0), lines_ref[1])
    swept = jnp.zeros((points, LANES), jnp.float32)
    for i in range(couples):
        rows = slice(i * points, (i + 1) * points)
        modes = sine_planes(jnp.concatenate([even[rows], odd[rows]], 1), planes_ref[...])
        swept = (modes[:, :LANES] + swept) * ratios_ref[2 * i]
        kept[2 * i] = swept
        swept = (modes[:, LANES:] + swept) * ratios_ref[2 * i + 1]
        if i < couples - 1:
            kept[2 * i + 1] = swept
    solved = (swept + ratios_ref[last] * pltpu.roll(swept, points, 1)) * middle_ref[...]
    even, odd = [], []
    for i in reversed(range(couples)):
        if i < couples - 1:
            solved = kept[2 * i + 1] + ratios_ref[2 * i + 1] * solved
        later = solved
        solved = kept[2 * i] + ratios_ref[2 * i] * later
        grid = sine_planes(jnp.concatenate([solved, later], 1), planes_ref[...])
        even.append(grid[:, :LANES])
        odd.append(grid[:, LANES:])
    even = sine_lines(jnp.concatenate(even, 0), lines_ref[0])
    odd = sine_lines(jnp.concatenate(odd, 0), lines_ref[1])
    for place, i in enumerate(reversed(range(couples))):
        rows = slice(place * points, (place + 1) * points)
        give(i, jnp.where(first_half, even[rows], odd[rows]))
        give(last - i, jnp.where(first_half, odd[rows], even[rows]))


def visit_kernel(choices, fresh, with_own, points, *refs):
    refs = list(refs)
    places_ref, lists_ref, own_ref = refs[:3]
    sources, at = [], 3
    for count in choices:
        sources.append(refs[at : at + count])
        at += count
    if not fresh:
        before_ref = refs[at]
        at += 1
    lines_ref, planes_ref, ratios_ref, middle_ref, totals, window, kept, extra, items, sems = refs[at:]
    own_count = own_ref.shape[0]
    slots = lists_ref.shape[1] - 1
    blocks = len(choices)

    def brought(slot, source):
        return pltpu.make_async_copy(source, window.at[pl.ds((slot + 1) * own_count, own_count)], sems.at[slot + 1])

    own_copy = pltpu.make_async_copy(own_ref, window.at[pl.ds(0, own_count)], sems.at[0])
    own_copy.start()
    for slot in range(blocks):
        for choice, source in enumerate(sources[slot]):
            if len(sources[slot]) == 1:
                brought(slot, source).start()
            else:
                @pl.when(places_ref[slot, 1] == choice)
                def _():
                    brought(slot, source).start()
    if fresh:
        totals[...] = jnp.zeros_like(totals)
    else:
        before = pltpu.make_async_copy(before_ref, totals, sems.at[blocks + 1])
        before.start()

    def note(keep, filled, own, other):
        @pl.when(keep)
        def _():
            items[filled, 0] = own
            items[filled, 1] = other

        return filled + keep.astype(jnp.int32)

    filled = jnp.int32(0)
    if with_own:
        def add_own(row, filled):
            keep = (row < lists_ref[0, slots, 0]) & (lists_ref[0, row, 1] < own_count)
            return note(keep, filled, lists_ref[0, row, 0], lists_ref[0, row, 1])

        filled = lax.fori_loop(0, slots, add_own, filled)
    for slot in range(blocks):
        offset = places_ref[slot, 0]
        start = (slot + 1) * own_count
        ahead = offset > 0
        which = jnp.where(ahead, 0, jnp.minimum(-offset, REACH))
        distance = jnp.abs(offset)

        def add_block(row, filled):
            keep = (row < lists_ref[which, slots, 0]) & (lists_ref[which, row, 1] // own_count == distance)
            lead = lists_ref[which, row, 0]
            follow = lists_ref[which, row, 1] - distance * own_count
            return note(keep, filled, jnp.where(ahead, lead, follow), start + jnp.where(ahead, follow, lead))

        filled = lax.fori_loop(0, slots, add_block, filled)

    own_copy.wait()
    for slot in range(blocks):
        brought(slot, sources[slot][0]).wait()
    if not fresh:
        before.wait()

    def visit(item, carried):
        mine = items[item, 0]
        other = items[item, 1]

        def load_mine(index):
            return window[mine, :, tile(index)]

        def load_other(index):
            return window[other, :, tile(index)]

        def give(index, potential):
            totals[mine, :, tile(index)] -= potential * load_other(index).astype(jnp.float32)
            if with_own:
                extra[:, tile(index)] = potential

        potential_tiles(
            load_mine, load_other, give, lines_ref, planes_ref, ratios_ref, middle_ref, kept, points
        )
        if with_own:
            @pl.when((other < own_count) & (other != mine))
            def _():
                def give_back(index, carried):
                    totals[other, :, tile(index)] -= extra[:, tile(index)] * load_mine(index).astype(jnp.float32)
                    return carried

                lax.fori_loop(0, points // 2, give_back, 0)

        return carried

    lax.fori_loop(0, filled, visit, 0)


def visit_blocks(places, lists, own, sources, before, constants, with_own):
    own_count, points, area = own.shape
    choices = tuple(len(source) for source in sources)
    flat = [array for source in sources for array in source]
    blocks = len(choices)
    vmem = pl.BlockSpec(memory_space=pltpu.VMEM)
    smem = pl.BlockSpec(memory_space=pltpu.SMEM)
    hbm = pl.BlockSpec(memory_space=pl.ANY)
    fresh = before is None
    most = (lists.shape[1] - 1) * (blocks + 1)
    pairs = 5
    return pl.pallas_call(
        functools.partial(visit_kernel, choices, fresh, with_own, points),
        out_shape=jax.ShapeDtypeStruct(own.shape, jnp.float32),
        in_specs=[smem, smem, hbm] + [hbm] * len(flat) + ([] if fresh else [hbm]) + [vmem] * len(constants),
        out_specs=vmem,
        scratch_shapes=[
            pltpu.VMEM(((blocks + 1) * own_count, points, area), jnp.bfloat16),
            pltpu.VMEM((points // 2, points, LANES), jnp.float32),
            pltpu.VMEM((points, area) if with_own else (8, LANES), jnp.float32),
            pltpu.SMEM((most, 2), jnp.int32),
            pltpu.SemaphoreType.DMA((blocks + 2,)),
        ],
        compiler_params=pltpu.CompilerParams(vmem_limit_bytes=48 * 2**20),
        cost_estimate=pl.CostEstimate(
            flops=pairs * 8 * points * points * points * points * 8, bytes_accessed=16 * 2**20, transcendentals=0
        ),
    )(places, lists, own, *flat, *([] if fresh else [before]), *constants)


def shards(orbitals, pair_list, pair_counts):
    count = lax.axis_size("orb")
    table = routes(count)
    device = lax.axis_index("orb")
    chip = (device % GROUP) // 2
    core = device % 2

    def send(value, name):
        return lax.ppermute(value, "orb", table[name])

    def placed(name, alternatives=1):
        held = jnp.array(HELD[name], jnp.int32)[chip]
        taker = jnp.array(TAKER[name], jnp.int32)[chip]
        offset = held - 2 * chip - core
        if name in ("y1", "y2"):
            return jnp.stack([jnp.where(core == taker, offset, NOWHERE), 0])
        choice = (core != taker).astype(jnp.int32)
        if name in ("x3", "y3"):
            choice = choice + 2 * jnp.array((1, 0, 0, 1), jnp.int32)[chip]
        return jnp.stack([offset, choice])

    listed = jnp.concatenate([pair_list, jnp.broadcast_to(pair_counts[:, None], (1, 2))], 0)
    behind = [
        lax.ppermute(listed, "orb", [(d, (d + distance) % count) for d in range(count)])
        for distance in range(1, REACH + 1)
    ]
    constants = [jnp.asarray(t) for t in tables(orbitals.shape[1])]

    partner = send(orbitals, "core")
    x1 = send(orbitals, "x1")
    y1 = send(orbitals, "y1")
    z1 = send(orbitals, "z1")
    lists = jnp.stack([listed] + behind)
    places = jnp.stack([1 - 2 * core, 0])[None]
    totals = visit_blocks(places, lists, orbitals, [[partner]], None, constants, True)

    held, x1, y1, z1 = lax.optimization_barrier((orbitals, x1, y1, z1))
    x2 = send(held, "x2")
    y2 = send(z1, "y2")
    z2 = send(x1, "z2")
    x1s = send(x1, "x1s")
    places = jnp.stack([placed("x1"), placed("y1")])
    totals = visit_blocks(places, lists, orbitals, [[x1, x1s], [y1]], totals, constants, False)

    x1, y1, x2, y2, z2 = lax.optimization_barrier((x1, y1, x2, y2, z2))
    x3a = send(y1, "x3a")
    x3b = send(y2, "x3b")
    y3a = send(x1, "y3a")
    y3b = send(z2, "y3b")
    x2s = send(x2, "x2s")
    places = jnp.stack([placed("x2"), placed("y2")])
    totals = visit_blocks(places, lists, orbitals, [[x2, x2s], [y2]], totals, constants, False)

    x3 = [x3a, send(x3a, "x3as"), x3b, send(x3b, "x3bs")]
    y3 = [y3a, send(y3a, "y3as"), y3b, send(y3b, "y3bs")]
    places = jnp.stack([placed("x3"), placed("y3")])
    return visit_blocks(places, lists, orbitals, [x3, y3], totals, constants, False)


def solution(mesh):
    return jax.shard_map(
        shards,
        mesh=mesh,
        in_specs=(P("orb", None, None), P("orb", None), P("orb")),
        out_specs=P("orb", None, None),
        check_vma=False,
    )
```

time: 1330 us -> 197 us (0.15)
  the two profiles are of different devices: /device:TPU:17 before, /device:TPU:8 now
where the time goes in v1:
time: 197 us
  Pallas kernels  68.7 us (35%)
  waiting for transfers between devices  56.4 us (29%)
  starting transfers between devices  40 us (20%)
  local copies, waits for them, and re-layouts  23.8 us (12%)
  between operations  7.78 us (4%)
    pallas_call x4, Pallas kernels, visit_blocks(): pl.pallas_call(functools.partial(visit_kernel, choices, fresh, with_own,...  68.7 us
    ppermute x17, waiting for transfers between devices, send(): return lax.ppermute(value, 'orb', table[name])  54.6 us
    ppermute x17, starting transfers between devices, send(): return lax.ppermute(value, 'orb', table[name])  37.5 us
    unnamed x24, local copies, waits for them, and re-layouts  8.2 us
    dynamic_slice x6, local copies, waits for them, and re-layouts, placed(): held = jnp.array(HELD[name], jnp.int32)[chip]  7.56 us
    dynamic_slice x4, local copies, waits for them, and re-layouts, placed(): taker = jnp.array(TAKER[name], jnp.int32)[chip]  5.01 us
  transfers between devices with their start and end apart: 20, of which 7 were waited for; matrix products, arithmetic and copies ran while one was open for 8% of the time, Pallas kernels for 25%

profile of v1, /device:TPU:8, one launch (start us, length us, event | category | flops | bytes accessed | tf_op | source)
XLA Modules:
  0.0 197.0 jit_solution(11418136277176980326)
XLA Ops:
  0.0 1.3 collective-permute-start.3
  1.3 2.0 %collective-permute-start.4 = (bf16[4,64,4096]{2,1,0:T(8,128)(2,1)}, bf16[4,64,4096]{2,1,0:T(8,128)(2,1)}, u32[]{:S(2)}, u32[]{:S(2)}) collective-permute-start(bf16[4,64,4096]{2,1,0:T(8,128)(2,1)} %refs_2_.7), channel_id=1, source_target_pairs={{1,4},{3,6},{4,1},{6,3},{9,12},{11,14},{12,9},{14,11},{17,20},{19,... | collective-permute-start | bytes 6291464 | tf_op jit(solution)/shard_map/ppermute | solution.py:303
  3.3 1.9 collective-permute-start.5
  5.2 23.0 %collective-permute-done.3.refs_3_ = bf16[4,64,4096]{2,1,0:T(8,128)(2,1)} collective-permute-done((bf16[4,64,4096]{2,1,0:T(8,128)(2,1)}, bf16[4,64,4096]{2,1,0:T(8,128)(2,1)}, u32[]{:S(2)}, u32[]{:S(2)}) %collective-permute-start.3) | collective-permute-done | bytes 2097184 | tf_op jit(solution)/shard_map/ppermute | solution.py:303
  28.2 3.2 %collective-permute-done.5 = bf16[4,64,4096]{2,1,0:T(8,128)(2,1)S(1)} collective-permute-done((bf16[4,64,4096]{2,1,0:T(8,128)(2,1)}, bf16[4,64,4096]{2,1,0:T(8,128)(2,1)S(1)}, u32[]{:S(2)}, u32[]{:S(2)}) %collective-permute-start.5) | collective-permute-done | bytes 2097184 | tf_op jit(solution)/shard_map/ppermute | solution.py:303
  31.4 2.0 %collective-permute-start.8 = (bf16[4,64,4096]{2,1,0:T(8,128)(2,1)}, bf16[4,64,4096]{2,1,0:T(8,128)(2,1)}, u32[]{:S(2)}, u32[]{:S(2)}) collective-permute-start(bf16[4,64,4096]{2,1,0:T(8,128)(2,1)} %collective-permute-done.3.refs_3_), channel_id=1, source_target_pairs={{4,12},{3,27},{12,20},{11,3},{20,28},{19,11},{28,4},{27,19}} | collective-permute-start | bytes 6291464 | tf_op jit(solution)/shard_map/ppermute | solution.py:303
  33.5 7.2 %collective-permute-start.6 = (bf16[4,64,4096]{2,1,0:T(8,128)(2,1)}, bf16[4,64,4096]{2,1,0:T(8,128)(2,1)}, u32[]{:S(2)}, u32[]{:S(2)}) collective-permute-start(bf16[4,64,4096]{2,1,0:T(8,128)(2,1)} %refs_2_.7), channel_id=1, source_target_pairs={{0,2},{3,1},{4,6},{7,5},{8,10},{11,9},{12,14},{15,13},{16,18},{19,... | collective-permute-start | bytes 6291464 | tf_op jit(solution)/shard_map/ppermute | solution.py:303
  40.7 1.9 collective-permute-start.7
  42.7 3.7 %collective-permute-start.18 = (bf16[4,64,4096]{2,1,0:T(8,128)(2,1)}, bf16[4,64,4096]{2,1,0:T(8,128)(2,1)}, u32[]{:S(2)}, u32[]{:S(2)}) collective-permute-start(bf16[4,64,4096]{2,1,0:T(8,128)(2,1)} %collective-permute-done.3.refs_3_), channel_id=1, source_target_pairs={{3,2},{0,1},{7,6},{4,5},{11,10},{8,9},{15,14},{12,13},{19,18},{16,... | collective-permute-start | bytes 6291464 | tf_op jit(solution)/shard_map/ppermute | solution.py:303
  47.8 15.5 %collective-permute-done.6.refs_3_ = bf16[4,64,4096]{2,1,0:T(8,128)(2,1)} collective-permute-done((bf16[4,64,4096]{2,1,0:T(8,128)(2,1)}, bf16[4,64,4096]{2,1,0:T(8,128)(2,1)}, u32[]{:S(2)}, u32[]{:S(2)}) %collective-permute-start.6) | collective-permute-done | bytes 2097184 | tf_op jit(solution)/shard_map/ppermute | solution.py:303
  63.2 2.5 %collective-permute-start.1 = (s32[17,2]{0,1:T(2,128)S(1)}, s32[17,2]{0,1:T(2,128)S(1)}, u32[]{:S(2)}, u32[]{:S(2)}) collective-permute-start(s32[17,2]{0,1:T(2,128)S(1)} %concatenate.3), channel_id=1, source_target_pairs={{0,2},{1,3},{2,4},{3,5},{4,6},{5,7},{6,8},{7,9},{8,10},{9,11},{10,... | collective-permute-start | bytes 416 | tf_op jit(solution)/shard_map/ppermute | solution.py:318
  65.7 2.5 %collective-permute-done.7.refs_5_ = bf16[4,64,4096]{2,1,0:T(8,128)(2,1)} collective-permute-done((bf16[4,64,4096]{2,1,0:T(8,128)(2,1)S(1)}, bf16[4,64,4096]{2,1,0:T(8,128)(2,1)}, u32[]{:S(2)}, u32[]{:S(2)}) %collective-permute-start.7) | collective-permute-done | bytes 2097184 | tf_op jit(solution)/shard_map/ppermute | solution.py:303
  68.2 1.3 collective-permute-start.11
  70.3 1.8 collective-permute-done.2
  72.1 3.4 %collective-permute-start.13 = (bf16[4,64,4096]{2,1,0:T(8,128)(2,1)}, bf16[4,64,4096]{2,1,0:T(8,128)(2,1)}, u32[]{:S(2)}, u32[]{:S(2)}) collective-permute-start(bf16[4,64,4096]{2,1,0:T(8,128)(2,1)} %collective-permute-done.3.refs_3_), channel_id=1, source_target_pairs={{0,4},{7,3},{8,12},{15,11},{16,20},{23,19},{24,28},{31,27}} | collective-permute-start | bytes 6291464 | tf_op jit(solution)/shard_map/ppermute | solution.py:303
  75.4 1.3 copy-done.10
  76.7 1.3 collective-permute-start.15
  78.0 1.3 collective-permute-start.17
  87.8 8.6 %collective-permute-done.11.refs_5_ = bf16[4,64,4096]{2,1,0:T(8,128)(2,1)} collective-permute-done((bf16[4,64,4096]{2,1,0:T(8,128)(2,1)}, bf16[4,64,4096]{2,1,0:T(8,128)(2,1)}, u32[]{:S(2)}, u32[]{:S(2)}) %collective-permute-start.11) | collective-permute-done | bytes 2097184 | tf_op jit(solution)/shard_map/ppermute | solution.py:303
  96.4 2.7 %collective-permute-start.12 = (bf16[4,64,4096]{2,1,0:T(8,128)(2,1)}, bf16[4,64,4096]{2,1,0:T(8,128)(2,1)}, u32[]{:S(2)}, u32[]{:S(2)}) collective-permute-start(bf16[4,64,4096]{2,1,0:T(8,128)(2,1)} %collective-permute-done.11.refs_5_), channel_id=1, source_target_pairs={{0,1},{7,6},{8,9},{15,14},{16,17},{23,22},{24,25},{31,30}} | collective-permute-start | bytes 6291464 | tf_op jit(solution)/shard_map/ppermute | solution.py:303
  99.1 2.1 %collective-permute-start.10 = (bf16[4,64,4096]{2,1,0:T(8,128)(2,1)S(1)}, bf16[4,64,4096]{2,1,0:T(8,128)(2,1)}, u32[]{:S(2)}, u32[]{:S(2)}) collective-permute-start(bf16[4,64,4096]{2,1,0:T(8,128)(2,1)S(1)} %collective-permute-done.9.refs_3_), channel_id=1, source_target_pairs={{3,2},{4,5},{11,10},{12,13},{19,18},{20,21},{27,26},{28,29}} | collective-permute-start | bytes 6291464 | tf_op jit(solution)/shard_map/ppermute | solution.py:303
  101.1 2.0 %collective-permute-start.14 = (bf16[4,64,4096]{2,1,0:T(8,128)(2,1)}, bf16[4,64,4096]{2,1,0:T(8,128)(2,1)}, u32[]{:S(2)}, u32[]{:S(2)}) collective-permute-start(bf16[4,64,4096]{2,1,0:T(8,128)(2,1)} %collective-permute-done.13.refs_7_), channel_id=1, source_target_pairs={{4,5},{3,2},{12,13},{11,10},{20,21},{19,18},{28,29},{27,26}} | collective-permute-start | bytes 6291464 | tf_op jit(solution)/shard_map/ppermute | solution.py:303
  103.1 1.8 collective-permute-done.15.refs_9_
  105.0 2.6 %collective-permute-start.16 = (bf16[4,64,4096]{2,1,0:T(8,128)(2,1)}, bf16[4,64,4096]{2,1,0:T(8,128)(2,1)}, u32[]{:S(2)}, u32[]{:S(2)}) collective-permute-start(bf16[4,64,4096]{2,1,0:T(8,128)(2,1)} %collective-permute-done.15.refs_9_), channel_id=1, source_target_pairs={{0,1},{7,6},{8,9},{15,14},{16,17},{23,22},{24,25},{31,30}} | collective-permute-start | bytes 6291464 | tf_op jit(solution)/shard_map/ppermute | solution.py:303
  115.0 1.3 dynamic_slice.45
  117.0 1.3 dynamic_slice.44
  121.3 1.6 copy-done
  126.6 1.6 copy-done.11
  128.2 16.9 %shard_map.199.refs_6_ = f32[4,64,4096]{2,1,0:T(8,128)} custom-call(s32[1,2]{1,0:T(1,128)S(1)} %get-tuple-element.26.refs_0_, s32[4,17,2]{2,1,0:T(8,128)S(1)} %pad_add_fusion.refs_1_, bf16[4,64,4096]{2,1,0:T(8,128)(2,1)S(1)} %copy-done, bf16[4,64,4096]{2,1,0:T(8,128)(2,1)S(1)} %copy-done.11, bf16[2,256,256]{2,1,0:T(8,128)(2,1)S(1)} %copy-done.4, ...), custom_call_target="tpu_custom_call" | custom-call | flops 5368709120 | bytes 16777216 | tf_op jit(solution)/shard_map/pallas_call | solution.py:276
  145.2 15.6 %shard_map.200.refs_6_ = f32[4,64,4096]{2,1,0:T(8,128)} custom-call(s32[2,2]{1,0:T(2,128)S(1)} %pad_add_fusion.3.refs_0_, s32[4,17,2]{2,1,0:T(8,128)S(1)} %pad_add_fusion.refs_1_, bf16[4,64,4096]{2,1,0:T(8,128)(2,1)S(1)} %copy-done.1, bf16[4,64,4096]{2,1,0:T(8,128)(2,1)} %collective-permute-done.3.refs_3_, ...), custom_call_target="tpu_custom_call" | custom-call | flops 5368709120 | bytes 16777216 | tf_op jit(solution)/shard_map/pallas_call | solution.py:276
  160.7 17.2 %shard_map.201.refs_11_ = f32[4,64,4096]{2,1,0:T(8,128)} custom-call(s32[2,2]{1,0:T(2,128)S(1)} %pad_add_fusion.2.refs_0_, s32[4,17,2]{2,1,0:T(8,128)S(1)} %pad_add_fusion.refs_1_, bf16[4,64,4096]{2,1,0:T(8,128)(2,1)S(1)} %copy-done.1, bf16[4,64,4096]{2,1,0:T(8,128)(2,1)} %collective-permute-done.6.refs_3_, ...), custom_call_target="tpu_custom_call" | custom-call | flops 5368709120 | bytes 16777216 | tf_op jit(solution)/shard_map/pallas_call | solution.py:276
  178.0 19.0 %shard_map.202 = f32[4,64,4096]{2,1,0:T(8,128)} custom-call(s32[2,2]{1,0:T(2,128)S(1)} %pad_add_fusion.1.refs_0_, s32[4,17,2]{2,1,0:T(8,128)S(1)} %pad_add_fusion.refs_1_, bf16[4,64,4096]{2,1,0:T(8,128)(2,1)S(1)} %copy-done.1, bf16[4,64,4096]{2,1,0:T(8,128)(2,1)S(1)} %collective-permute-done.9.refs_3_, bf16[4,64,4096]{2,1,0:T(8,128)(2,1)} %collective-permute-done.10.refs_4_, ...), custom_call_target="tpu_custom_call" | custom-call | flops 5368709120 | bytes 16777216 | tf_op jit(solution)/shard_map/pallas_call | solution.py:276
  (61 shorter events, 18.0 us)
Async XLA Ops:
  0.0 28.2 %collective-permute-start.3 = (bf16[4,64,4096]{2,1,0:T(8,128)(2,1)}, bf16[4,64,4096]{2,1,0:T(8,128)(2,1)}, u32[]{:S(2)}, u32[]{:S(2)}) collective-permute-start(bf16[4,64,4096]{2,1,0:T(8,128)(2,1)} %refs_2_.7), channel_id=1, source_target_pairs={{1,3},{2,0},{5,7},{6,4},{9,11},{10,8},{13,15},{14,12},{17,19},{18,... | collective-permute-start | bytes 6291464 | tf_op jit(solution)/shard_map/ppermute | solution.py:303
  1.3 26.9 %collective-permute-start.4 = (bf16[4,64,4096]{2,1,0:T(8,128)(2,1)}, bf16[4,64,4096]{2,1,0:T(8,128)(2,1)}, u32[]{:S(2)}, u32[]{:S(2)}) collective-permute-start(bf16[4,64,4096]{2,1,0:T(8,128)(2,1)} %refs_2_.7), channel_id=1, source_target_pairs={{1,4},{3,6},{4,1},{6,3},{9,12},{11,14},{12,9},{14,11},{17,20},{19,... | collective-permute-start | bytes 6291464 | tf_op jit(solution)/shard_map/ppermute | solution.py:303
  3.3 28.1 %collective-permute-start.5 = (bf16[4,64,4096]{2,1,0:T(8,128)(2,1)}, bf16[4,64,4096]{2,1,0:T(8,128)(2,1)S(1)}, u32[]{:S(2)}, u32[]{:S(2)}) collective-permute-start(bf16[4,64,4096]{2,1,0:T(8,128)(2,1)} %refs_2_.7), channel_id=1, source_target_pairs={{0,24},{2,26},{5,13},{7,15},{8,0},{10,2},{13,21},{15,23},{16,8},{1... | collective-permute-start | bytes 6291464 | tf_op jit(solution)/shard_map/ppermute | solution.py:303
  31.4 16.3 %collective-permute-start.8 = (bf16[4,64,4096]{2,1,0:T(8,128)(2,1)}, bf16[4,64,4096]{2,1,0:T(8,128)(2,1)}, u32[]{:S(2)}, u32[]{:S(2)}) collective-permute-start(bf16[4,64,4096]{2,1,0:T(8,128)(2,1)} %collective-permute-done.3.refs_3_), channel_id=1, source_target_pairs={{4,12},{3,27},{12,20},{11,3},{20,28},{19,11},{28,4},{27,19}} | collective-permute-start | bytes 6291464 | tf_op jit(solution)/shard_map/ppermute | solution.py:303
  33.5 29.7 %collective-permute-start.6 = (bf16[4,64,4096]{2,1,0:T(8,128)(2,1)}, bf16[4,64,4096]{2,1,0:T(8,128)(2,1)}, u32[]{:S(2)}, u32[]{:S(2)}) collective-permute-start(bf16[4,64,4096]{2,1,0:T(8,128)(2,1)} %refs_2_.7), channel_id=1, source_target_pairs={{0,2},{3,1},{4,6},{7,5},{8,10},{11,9},{12,14},{15,13},{16,18},{19,... | collective-permute-start | bytes 6291464 | tf_op jit(solution)/shard_map/ppermute | solution.py:303
  40.7 27.5 %collective-permute-start.7 = (bf16[4,64,4096]{2,1,0:T(8,128)(2,1)S(1)}, bf16[4,64,4096]{2,1,0:T(8,128)(2,1)}, u32[]{:S(2)}, u32[]{:S(2)}) collective-permute-start(bf16[4,64,4096]{2,1,0:T(8,128)(2,1)S(1)} %collective-permute-done.5), channel_id=1, source_target_pairs={{0,5},{2,7},{5,0},{7,2},{8,13},{10,15},{13,8},{15,10},{16,21},{18,... | collective-permute-start | bytes 6291464 | tf_op jit(solution)/shard_map/ppermute | solution.py:303
  42.6 32.8 %collective-permute-start.19 = (bf16[4,64,4096]{2,1,0:T(8,128)(2,1)}, bf16[4,64,4096]{2,1,0:T(8,128)(2,1)S(1)}, u32[]{:S(2)}, u32[]{:S(2)}) collective-permute-start(bf16[4,64,4096]{2,1,0:T(8,128)(2,1)} %refs_2_.7), channel_id=1, source_target_pairs={{0,1},{1,0},{2,3},{3,2},{4,5},{5,4},{6,7},{7,6},{8,9},{9,8},{10,11... | collective-permute-start | bytes 6291464 | tf_op jit(solution)/shard_map/ppermute | solution.py:303
  42.7 35.3 %collective-permute-start.18 = (bf16[4,64,4096]{2,1,0:T(8,128)(2,1)}, bf16[4,64,4096]{2,1,0:T(8,128)(2,1)}, u32[]{:S(2)}, u32[]{:S(2)}) collective-permute-start(bf16[4,64,4096]{2,1,0:T(8,128)(2,1)} %collective-permute-done.3.refs_3_), channel_id=1, source_target_pairs={{3,2},{0,1},{7,6},{4,5},{11,10},{8,9},{15,14},{12,13},{19,18},{16,... | collective-permute-start | bytes 6291464 | tf_op jit(solution)/shard_map/ppermute | solution.py:303
  47.8 20.4 %collective-permute-start = (s32[17,2]{0,1:T(2,128)S(1)}, s32[17,2]{0,1:T(2,128)S(1)}, u32[]{:S(2)}, u32[]{:S(2)}) collective-permute-start(s32[17,2]{0,1:T(2,128)S(1)} %concatenate.3), channel_id=1, source_target_pairs={{0,1},{1,2},{2,3},{3,4},{4,5},{5,6},{6,7},{7,8},{8,9},{9,10},{10,1... | collective-permute-start | bytes 416 | tf_op jit(solution)/shard_map/ppermute | solution.py:318
  63.2 6.2 %collective-permute-start.1 = (s32[17,2]{0,1:T(2,128)S(1)}, s32[17,2]{0,1:T(2,128)S(1)}, u32[]{:S(2)}, u32[]{:S(2)}) collective-permute-start(s32[17,2]{0,1:T(2,128)S(1)} %concatenate.3), channel_id=1, source_target_pairs={{0,2},{1,3},{2,4},{3,5},{4,6},{5,7},{6,8},{7,9},{8,10},{9,11},{10,... | collective-permute-start | bytes 416 | tf_op jit(solution)/shard_map/ppermute | solution.py:318
  68.2 3.9 %collective-permute-start.2 = (s32[17,2]{0,1:T(2,128)S(1)}, s32[17,2]{0,1:T(2,128)S(1)}, u32[]{:S(2)}, u32[]{:S(2)}) collective-permute-start(s32[17,2]{0,1:T(2,128)S(1)} %concatenate.3), channel_id=1, source_target_pairs={{0,3},{1,4},{2,5},{3,6},{4,7},{5,8},{6,9},{7,10},{8,11},{9,12},{10... | collective-permute-start | bytes 416 | tf_op jit(solution)/shard_map/ppermute | solution.py:318
  68.2 28.2 %collective-permute-start.11 = (bf16[4,64,4096]{2,1,0:T(8,128)(2,1)}, bf16[4,64,4096]{2,1,0:T(8,128)(2,1)}, u32[]{:S(2)}, u32[]{:S(2)}) collective-permute-start(bf16[4,64,4096]{2,1,0:T(8,128)(2,1)} %collective-permute-done.7.refs_5_), channel_id=1, source_target_pairs={{2,0},{5,7},{10,8},{13,15},{18,16},{21,23},{26,24},{29,31}} | collective-permute-start | bytes 6291464 | tf_op jit(solution)/shard_map/ppermute | solution.py:303
  69.5 29.6 %collective-permute-start.9 = (bf16[4,64,4096]{2,1,0:T(8,128)(2,1)}, bf16[4,64,4096]{2,1,0:T(8,128)(2,1)S(1)}, u32[]{:S(2)}, u32[]{:S(2)}) collective-permute-start(bf16[4,64,4096]{2,1,0:T(8,128)(2,1)} %collective-permute-done.4.refs_5_), channel_id=1, source_target_pairs={{1,3},{6,4},{9,11},{14,12},{17,19},{22,20},{25,27},{30,28}} | collective-permute-start | bytes 6291464 | tf_op jit(solution)/shard_map/ppermute | solution.py:303
  72.1 29.1 %collective-permute-start.13 = (bf16[4,64,4096]{2,1,0:T(8,128)(2,1)}, bf16[4,64,4096]{2,1,0:T(8,128)(2,1)}, u32[]{:S(2)}, u32[]{:S(2)}) collective-permute-start(bf16[4,64,4096]{2,1,0:T(8,128)(2,1)} %collective-permute-done.3.refs_3_), channel_id=1, source_target_pairs={{0,4},{7,3},{8,12},{15,11},{16,20},{23,19},{24,28},{31,27}} | collective-permute-start | bytes 6291464 | tf_op jit(solution)/shard_map/ppermute | solution.py:303
  75.4 1.3 copy-start.10
  76.7 28.2 %collective-permute-start.15 = (bf16[4,64,4096]{2,1,0:T(8,128)(2,1)}, bf16[4,64,4096]{2,1,0:T(8,128)(2,1)}, u32[]{:S(2)}, u32[]{:S(2)}) collective-permute-start(bf16[4,64,4096]{2,1,0:T(8,128)(2,1)} %collective-permute-done.8), channel_id=1, source_target_pairs={{4,0},{3,7},{12,8},{11,15},{20,16},{19,23},{28,24},{27,31}} | collective-permute-start | bytes 6291464 | tf_op jit(solution)/shard_map/ppermute | solution.py:303
  78.0 82.7 %collective-permute-start.17 = (bf16[4,64,4096]{2,1,0:T(8,128)(2,1)}, bf16[4,64,4096]{2,1,0:T(8,128)(2,1)}, u32[]{:S(2)}, u32[]{:S(2)}) collective-permute-start(bf16[4,64,4096]{2,1,0:T(8,128)(2,1)} %collective-permute-done.6.refs_3_), channel_id=1, source_target_pairs={{2,3},{1,0},{6,7},{5,4},{10,11},{9,8},{14,15},{13,12},{18,19},{17,... | collective-permute-start | bytes 6291464 | tf_op jit(solution)/shard_map/ppermute | solution.py:303
  96.4 81.5 %collective-permute-start.12 = (bf16[4,64,4096]{2,1,0:T(8,128)(2,1)}, bf16[4,64,4096]{2,1,0:T(8,128)(2,1)}, u32[]{:S(2)}, u32[]{:S(2)}) collective-permute-start(bf16[4,64,4096]{2,1,0:T(8,128)(2,1)} %collective-permute-done.11.refs_5_), channel_id=1, source_target_pairs={{0,1},{7,6},{8,9},{15,14},{16,17},{23,22},{24,25},{31,30}} | collective-permute-start | bytes 6291464 | tf_op jit(solution)/shard_map/ppermute | solution.py:303
  99.1 78.9 %collective-permute-start.10 = (bf16[4,64,4096]{2,1,0:T(8,128)(2,1)S(1)}, bf16[4,64,4096]{2,1,0:T(8,128)(2,1)}, u32[]{:S(2)}, u32[]{:S(2)}) collective-permute-start(bf16[4,64,4096]{2,1,0:T(8,128)(2,1)S(1)} %collective-permute-done.9.refs_3_), channel_id=1, source_target_pairs={{3,2},{4,5},{11,10},{12,13},{19,18},{20,21},{27,26},{28,29}} | collective-permute-start | bytes 6291464 | tf_op jit(solution)/shard_map/ppermute | solution.py:303
  101.1 76.8 %collective-permute-start.14 = (bf16[4,64,4096]{2,1,0:T(8,128)(2,1)}, bf16[4,64,4096]{2,1,0:T(8,128)(2,1)}, u32[]{:S(2)}, u32[]{:S(2)}) collective-permute-start(bf16[4,64,4096]{2,1,0:T(8,128)(2,1)} %collective-permute-done.13.refs_7_), channel_id=1, source_target_pairs={{4,5},{3,2},{12,13},{11,10},{20,21},{19,18},{28,29},{27,26}} | collective-permute-start | bytes 6291464 | tf_op jit(solution)/shard_map/ppermute | solution.py:303
  105.0 73.0 %collective-permute-start.16 = (bf16[4,64,4096]{2,1,0:T(8,128)(2,1)}, bf16[4,64,4096]{2,1,0:T(8,128)(2,1)}, u32[]{:S(2)}, u32[]{:S(2)}) collective-permute-start(bf16[4,64,4096]{2,1,0:T(8,128)(2,1)} %collective-permute-done.15.refs_9_), channel_id=1, source_target_pairs={{0,1},{7,6},{8,9},{15,14},{16,17},{23,22},{24,25},{31,30}} | collective-permute-start | bytes 6291464 | tf_op jit(solution)/shard_map/ppermute | solution.py:303
  121.3 1.6 copy-start
  122.9 1.2 copy-start.2
  124.1 0.9 copy-start.4
  125.0 0.8 copy-start.6
  125.8 0.8 copy-start.8
  126.6 1.6 copy-start.11
  128.2 16.9 %copy-start.1 = (bf16[4,64,4096]{2,1,0:T(8,128)(2,1)S(1)}, bf16[4,64,4096]{2,1,0:T(8,128)(2,1)}, u32[]{:S(2)}) copy-start(bf16[4,64,4096]{2,1,0:T(8,128)(2,1)} %refs_2_.7) | copy-start | bytes 6291460
  128.2 17.0 %copy-start.3 = (f32[32,64,128]{2,1,0:T(8,128)S(1)}, f32[32,64,128]{2,1,0:T(8,128)}, u32[]{:S(2)}) copy-start(f32[32,64,128]{2,1,0:T(8,128)} %constant.81.clone.refs_6_.refs_9_.refs_14_) | copy-start | bytes 3145732
  128.2 17.0 %copy-start.5 = (bf16[2,256,256]{2,1,0:T(8,128)(2,1)S(1)}, bf16[2,256,256]{2,1,0:T(8,128)(2,1)}, u32[]{:S(2)}) copy-start(bf16[2,256,256]{2,1,0:T(8,128)(2,1)} %constant.79.clone.refs_4_.refs_7_.refs_12_) | copy-start | bytes 786436
  128.2 17.0 %copy-start.7 = (bf16[64,256]{1,0:T(8,128)(2,1)S(1)}, bf16[64,256]{1,0:T(8,128)(2,1)}, u32[]{:S(2)}) copy-start(bf16[64,256]{1,0:T(8,128)(2,1)} %constant.80.clone.refs_5_.refs_8_.refs_13_) | copy-start | bytes 98308
  128.2 17.0 %copy-start.9 = (f32[64,128]{1,0:T(8,128)S(1)}, f32[64,128]{1,0:T(8,128)}, u32[]{:S(2)}) copy-start(f32[64,128]{1,0:T(8,128)} %constant.82.clone.refs_7_.refs_10_.refs_15_) | copy-start | bytes 98308
